TPU v7x, 512 devices: a whole 4x8x8 slice. The times are simulated.
512 devices in a mesh: seq: 64 (over y, x, core), tp: 8 (over z).
Axes of the slice: x: 4, y: 8, z: 8, core: 2. Of those that a mesh axis runs over, the one named last changes fastest.
Arguments:
- queries: bfloat16 [32768, 4096], P('seq', 'tp'), may hold values from -9 to 9
- keys: bfloat16 [32768, 4096], P('seq', 'tp'), may hold values from -9 to 9
- values: bfloat16 [32768, 4096], P('seq', 'tp'), may hold values from -6 to 6
- route: int32 [32, 32768], P('tp', 'seq'), may hold values from 0 to 32767, as said below
- members: int32 [32, 32768], P('tp', 'seq'), may hold values from 0 to 32767, as said below
- pattern: int32 [32, 128, 10], P('tp', 'seq'), may hold values from 0 to 1, as said below
- w_out: bfloat16 [4096, 4096], P('tp', 'seq'), may hold values from -0.25 to 0.25
Outputs:
- mixed: bfloat16 [32768, 4096], P('seq', 'tp')
Inputs may be any that keep to these rules, and one draw needn't show every extreme that they name: `route`: each row is a permutation of the positions; for every aligned block of 512 positions and every aligned block of 512 slots, exactly 8 of the block's positions have their slot in that slot block. members[h] is the inverse permutation of route[h]: members[h, route[h, p]] = p. `pattern`: entries 2 * 2 and 2 * 2 + 1 (the cluster's own blocks) are always 1; entries whose cluster lies outside 0 to 127 are always 0.
All inputs are finite; a program needn't handle non-finite values.
Results may differ from a plain program's by a relative error of at most 0.017.
Values may be sent and summed in bfloat16 or wider, within the bound.
A program may use at most 64 MiB of HBM per device.

v0:
```python
import jax
import jax.numpy as jnp
from jax import lax
from jax.sharding import PartitionSpec as P

CLUSTER = 256
REACH = 2


def extended_2(cells, sides, width):
    for axis, dim in sides:
        count = lax.axis_size(axis)
        ends = count - 1
        head = lax.slice_in_dim(cells, 0, width, axis=dim)
        tail = lax.slice_in_dim(cells, cells.shape[dim] - width, cells.shape[dim], axis=dim)
        cells = jnp.concatenate(
            [
                lax.ppermute(tail, axis, [(i, (i + 1) % count) for i in range(ends)]),
                cells,
                lax.ppermute(head, axis, [((i + 1) % count, i) for i in range(ends)]),
            ],
            axis=dim,
        )
    return cells


def attend_head(pieces):
    query_rows, key_rows, value_rows, pattern_rows = pieces
    head_width = query_rows.shape[1]
    cluster_count = query_rows.shape[0] // CLUSTER
    window_rows = (2 * REACH + 1) * CLUSTER
    starts = jnp.arange(cluster_count) * CLUSTER
    key_window = jax.vmap(
        lambda slot_start: lax.dynamic_slice_in_dim(key_rows, slot_start, window_rows, 0)
    )(starts)
    value_window = jax.vmap(
        lambda slot_start: lax.dynamic_slice_in_dim(value_rows, slot_start, window_rows, 0)
    )(starts)
    query_blocks = query_rows.reshape(cluster_count, CLUSTER, head_width)
    scores = jnp.einsum(
        "cqd,ckd->cqk", query_blocks, key_window, preferred_element_type=jnp.float32
    ) * head_width ** (-0.5)
    allowed = jnp.repeat(pattern_rows, CLUSTER // 2, axis=1) > 0
    scores = jnp.where(allowed[:, None, :], scores, -jnp.inf)
    row_max = jnp.max(scores, axis=-1, keepdims=True)
    exponent = jnp.exp(scores - row_max)
    weights = (exponent / jnp.sum(exponent, axis=-1, keepdims=True)).astype(jnp.bfloat16)
    context = jnp.einsum(
        "cqk,ckd->cqd", weights, value_window, preferred_element_type=jnp.float32
    ).astype(jnp.bfloat16)
    return context.reshape(query_rows.shape[0], head_width)


def buffer_index(group_of, order_key, per_peer):
    same_group = group_of[:, :, None] == group_of[:, None, :]
    earlier = order_key[:, None, :] < order_key[:, :, None]
    rank = jnp.sum((same_group & earlier).astype(jnp.int32), axis=2)
    return group_of * per_peer + rank


def shards(queries, keys, values, route, members, pattern, w_out):
    rows_here = queries.shape[0]
    head_count = route.shape[0]
    head_width = queries.shape[1] // head_count
    peer_count = lax.axis_size("seq")
    per_peer = rows_here // peer_count
    local_iota = jnp.arange(rows_here, dtype=jnp.int32)
    send_index = buffer_index(route // rows_here, route, per_peer)
    local_slots = jnp.broadcast_to(local_iota[None, :], members.shape)
    arrival_index = buffer_index(members // rows_here, local_slots, per_peer)
    send_table = (send_index[:, None, :] == local_iota[None, :, None]).astype(jnp.bfloat16)
    land_table = (arrival_index[:, :, None] == local_iota[None, None, :]).astype(jnp.bfloat16)
    stacked = jnp.concatenate(
        [
            queries.reshape(rows_here, head_count, head_width),
            keys.reshape(rows_here, head_count, head_width),
            values.reshape(rows_here, head_count, head_width),
        ],
        axis=2,
    )
    packed = jnp.einsum(
        "hap,phd->had", send_table, stacked, preferred_element_type=jnp.float32
    ).astype(jnp.bfloat16)

    def outgoing(column_index):
        part_rows = packed[:, :, column_index * head_width : (column_index + 1) * head_width]
        return part_rows.reshape(head_count, peer_count, per_peer, head_width)

    sent_query, sent_key, sent_value = (
        lax.all_to_all(outgoing(0), "seq", split_axis=1, concat_axis=1, tiled=True),
        lax.all_to_all(outgoing(1), "seq", split_axis=1, concat_axis=1, tiled=True),
        lax.all_to_all(outgoing(2), "seq", split_axis=1, concat_axis=1, tiled=True),
    )
    arrived = jnp.concatenate(
        [
            sent_query.reshape(head_count, rows_here, head_width),
            sent_key.reshape(head_count, rows_here, head_width),
            sent_value.reshape(head_count, rows_here, head_width),
        ],
        axis=2,
    )
    placed = jnp.einsum(
        "hsa,had->hsd", land_table, arrived, preferred_element_type=jnp.float32
    ).astype(jnp.bfloat16)
    ordered_query = placed[:, :, :head_width]
    keys_values = jnp.stack(
        [placed[:, :, head_width : 2 * head_width], placed[:, :, 2 * head_width :]]
    )
    extended = extended_2(keys_values, (("seq", 2),), REACH * CLUSTER)
    context = lax.map(attend_head, (ordered_query, extended[0], extended[1], pattern))
    returning = jnp.einsum(
        "hsa,hsd->had", land_table, context, preferred_element_type=jnp.float32
    ).astype(jnp.bfloat16)
    returning = returning.reshape(head_count, peer_count, per_peer, head_width)
    returned = lax.all_to_all(returning, "seq", split_axis=1, concat_axis=1, tiled=True).reshape(
        head_count, rows_here, head_width
    )
    attended = jnp.einsum(
        "hap,had->phd", send_table, returned, preferred_element_type=jnp.float32
    ).astype(jnp.bfloat16)
    attended = attended.reshape(rows_here, head_count * head_width)
    partial_value = jnp.dot(
        attended,
        lax.all_gather(w_out, "seq", axis=1, tiled=True),
        preferred_element_type=jnp.float32,
    )
    column_count = partial_value.shape[1] // lax.axis_size("tp")
    summed = lax.psum(partial_value.astype(jnp.bfloat16), "tp").astype(jnp.float32)
    mixed_out = lax.dynamic_slice_in_dim(
        summed, lax.axis_index("tp") * column_count, column_count, 1
    )
    return mixed_out.astype(jnp.bfloat16)


def solution(mesh):
    placed = (
        P("seq", "tp"),
        P("seq", "tp"),
        P("seq", "tp"),
        P("tp", "seq"),
        P("tp", "seq"),
        P("tp", "seq", None),
        P("tp", "seq"),
    )
    return jax.shard_map(
        shards, mesh=mesh, in_specs=placed, out_specs=P("seq", "tp"), check_vma=False
    )
```

profile of v0, /device:TPU:1, one launch (start us, length us, event | category | flops | bytes accessed | tf_op | source)
XLA Modules:
  0.0 320.6 jit_solution(11738363935786757012)
XLA Ops:
  6.5 0.8 add_select_fusion
  7.3 1.8 convert_reduce_fusion
  9.1 0.7 multiply_add_fusion
  9.9 1.3 copy.34
  11.4 1.3 copy.35
  13.4 1.3 fusion.22
  15.1 0.9 copy.44
  16.0 11.6 %all-to-all-start.2 = ((bf16[4,64,8,128]{3,2,0,1:T(8,128)(2,1)}), bf16[4,64,8,128]{3,2,0,1:T(8,128)(2,1)S(1)}, u32[]{:S(2)}, u32[]{:S(2)}) async-start(bf16[4,64,8,128]{3,2,0,1:T(8,128)(2,1)} %copy.44), calls=%async_computation.2 | async-start | bytes 1048576 | tf_op jit(solution)/shard_map/all_to_all | solution.py:92
  27.6 0.9 copy.42
  28.5 16.8 %all-to-all-done.2 = bf16[4,64,8,128]{3,2,0,1:T(8,128)(2,1)S(1)} async-done(((bf16[4,64,8,128]{3,2,0,1:T(8,128)(2,1)}), bf16[4,64,8,128]{3,2,0,1:T(8,128)(2,1)S(1)}, u32[]{:S(2)}, u32[]{:S(2)}) %all-to-all-start.2) | async-done | bytes 524320 | tf_op jit(solution)/shard_map/all_to_all | solution.py:92
  45.3 5.7 %all-to-all-start.1 = ((bf16[4,64,8,128]{3,2,0,1:T(8,128)(2,1)}), bf16[4,64,8,128]{3,2,0,1:T(8,128)(2,1)S(1)}, u32[]{:S(2)}, u32[]{:S(2)}) async-start(bf16[4,64,8,128]{3,2,0,1:T(8,128)(2,1)} %copy.42), calls=%async_computation.1 | async-start | bytes 1048576 | tf_op jit(solution)/shard_map/all_to_all | solution.py:91
  51.0 0.9 copy.40
  51.9 16.8 %all-to-all-done.1 = bf16[4,64,8,128]{3,2,0,1:T(8,128)(2,1)S(1)} async-done(((bf16[4,64,8,128]{3,2,0,1:T(8,128)(2,1)}), bf16[4,64,8,128]{3,2,0,1:T(8,128)(2,1)S(1)}, u32[]{:S(2)}, u32[]{:S(2)}) %all-to-all-start.1) | async-done | bytes 524320 | tf_op jit(solution)/shard_map/all_to_all | solution.py:91
  68.8 5.7 %all-to-all-start = ((bf16[4,64,8,128]{3,2,0,1:T(8,128)(2,1)}), bf16[4,64,8,128]{3,2,0,1:T(8,128)(2,1)S(1)}, u32[]{:S(2)}, u32[]{:S(2)}) async-start(bf16[4,64,8,128]{3,2,0,1:T(8,128)(2,1)} %copy.40), calls=%async_computation | async-start | bytes 1048576 | tf_op jit(solution)/shard_map/all_to_all | solution.py:90
  74.7 1.2 convert_reduce_fusion.1
  76.1 16.1 %all-to-all-done = bf16[4,64,8,128]{3,2,0,1:T(8,128)(2,1)S(1)} async-done(((bf16[4,64,8,128]{3,2,0,1:T(8,128)(2,1)}), bf16[4,64,8,128]{3,2,0,1:T(8,128)(2,1)S(1)}, u32[]{:S(2)}, u32[]{:S(2)}) %all-to-all-start) | async-done | bytes 524320 | tf_op jit(solution)/shard_map/all_to_all | solution.py:90
  92.3 1.3 fusion.21
  93.6 1.2 slice_bitcast_fusion.3
  94.9 3.4 %collective-permute-start = (bf16[2,4,512,128]{3,2,1,0:T(8,128)(2,1)S(1)}, bf16[2,4,512,128]{3,2,1,0:T(8,128)(2,1)S(1)}, u32[]{:S(2)}, u32[]{:S(2)}) collective-permute-start(bf16[2,4,512,128]{3,2,1,0:T(8,128)(2,1)S(1)} %pad_maximum_fusion.1), channel_id=1, source_target_pairs={{0,8},{8,16},{16,24},{24,32},{32,40},{40,48},{48,56},{56,64},{64,7... | collective-permute-start | bytes 3145736 | tf_op jit(solution)/shard_map/ppermute | solution.py:18
  98.3 1.9 collective-permute-start.1
  100.5 9.5 %collective-permute-done = bf16[2,4,512,128]{3,2,1,0:T(8,128)(2,1)S(1)} collective-permute-done((bf16[2,4,512,128]{3,2,1,0:T(8,128)(2,1)S(1)}, bf16[2,4,512,128]{3,2,1,0:T(8,128)(2,1)S(1)}, u32[]{:S(2)}, u32[]{:S(2)}) %collective-permute-start) | collective-permute-done | bytes 1048608 | tf_op jit(solution)/shard_map/ppermute | solution.py:18
  110.0 4.5 %collective-permute-done.1 = bf16[2,4,512,128]{3,2,1,0:T(8,128)(2,1)} collective-permute-done((bf16[2,4,512,128]{3,2,1,0:T(8,128)(2,1)S(1)}, bf16[2,4,512,128]{3,2,1,0:T(8,128)(2,1)}, u32[]{:S(2)}, u32[]{:S(2)}) %collective-permute-start.1) | collective-permute-done | bytes 1048608 | tf_op jit(solution)/shard_map/ppermute | solution.py:20
  114.5 1.3 pad_maximum_fusion
  115.8 1.4 slice_bitcast_fusion
  117.2 27.3 %while.16 = (s32[]{:T(128)}, bf16[4,512,128]{2,1,0:T(8,128)(2,1)}, s32[4,2,10]{2,1,0:T(2,128)}, bf16[4,512,128]{2,1,0:T(8,128)(2,1)}, bf16[4,1536,128]{2,1,0:T(8...) while((s32[]{:T(128)}, bf16[4,512,128]{2,1,0:T(8,128)(2,1)}, ...), condition=%wide.region_5.6_spmd, body=%wide.region_2.5_spmd.sunk | while | flops 509283360 | bytes 7096867 | solution.py:110
  117.2 1.1 dynamic-slice_bitcast_fusion.3
  118.8 0.9 constant_dynamic-slice_fusion.7
  120.5 1.0 fusion.65
  122.0 1.4 fusion.66
  124.0 1.0 dynamic-slice_bitcast_fusion.3
  125.6 0.9 constant_dynamic-slice_fusion.7
  127.3 1.0 fusion.65
  128.8 1.4 fusion.66
  130.9 1.0 dynamic-slice_bitcast_fusion.3
  132.4 0.9 constant_dynamic-slice_fusion.7
  134.1 1.0 fusion.65
  135.6 1.4 fusion.66
  137.7 1.1 dynamic-slice_bitcast_fusion.3
  139.3 0.9 constant_dynamic-slice_fusion.7
  141.0 1.0 fusion.65
  142.4 1.4 fusion.66
  144.5 1.8 fusion.35
  146.5 31.2 %all_to_all.20 = bf16[4,64,8,128]{3,2,0,1:T(8,128)(2,1)S(1)} all-to-all(bf16[4,64,8,128]{3,2,0,1:T(8,128)(2,1)S(1)} %copy.47), channel_id=1, replica_groups=mesh['seq'=64,'tp'=8] {'seq'}, dimensions={1} | all-to-all | bytes 1048576 | tf_op jit(solution)/shard_map/all_to_all | solution.py:115
  177.6 0.9 fusion.34
  178.6 11.8 %all-gather.2.cloned.1.call-done = bf16[512,4096]{0,1:T(8,128)(2,1)} async-done(((bf16[512,64]{0,1:T(8,128)(2,1)}), bf16[512,4096]{0,1:T(8,128)(2,1)}) %all-gather.2.cloned.1.call-update) | async-done | bytes 4194320 | tf_op jit(solution)/shard_map/all_gather | solution.py:124
  190.3 6.6 %convolution_convert_fusion = bf16[512,4096]{1,0:T(8,128)(2,1)} fusion(bf16[512,512]{0,1:T(8,128)(2,1)S(1)} %bitcast.112, bf16[512,4096]{0,1:T(8,128)(2,1)} %all-gather.2.cloned.1.call-done), kind=kOutput, calls=%fused_computation.26 | convolution fusion | flops 2149580800 | bytes 8912896 | tf_op jit(solution)/shard_map/dot_general | solution.py:122
  196.9 115.0 %all-reduce.3.cloned.1.call-done = bf16[512,4096]{1,0:T(8,128)(2,1)} async-done(((bf16[512,4096]{1,0:T(8,128)(2,1)}), bf16[512,4096]{1,0:T(8,128)(2,1)}) %all-reduce.3.cloned.1.call-update) | async-done | bytes 4194320 | tf_op jit(solution)/shard_map/psum | solution.py:128
  311.9 1.9 convert_convert_fusion
  (94 shorter events, 14.7 us)
Async XLA Ops:
  6.5 6.4 %copy-start = (bf16[512,512]{1,0:T(8,128)(2,1)S(1)}, bf16[512,512]{1,0:T(8,128)(2,1)}, u32[]{:S(2)}) copy-start(bf16[512,512]{1,0:T(8,128)(2,1)} %param.11) | copy-start | bytes 1572868
  15.1 59.6 %copy-start.1 = (s32[4,512]{1,0:T(4,128)S(1)}, s32[4,512]{1,0:T(4,128)}, u32[]{:S(2)}) copy-start(s32[4,512]{1,0:T(4,128)} %param.13) | copy-start | bytes 24580
  16.0 29.3 %all-to-all-start.2 = ((bf16[4,64,8,128]{3,2,0,1:T(8,128)(2,1)}), bf16[4,64,8,128]{3,2,0,1:T(8,128)(2,1)S(1)}, u32[]{:S(2)}, u32[]{:S(2)}) async-start(bf16[4,64,8,128]{3,2,0,1:T(8,128)(2,1)} %copy.44), calls=%async_computation.2 | async-start | bytes 1048576 | tf_op jit(solution)/shard_map/all_to_all | solution.py:92
  45.3 23.4 %all-to-all-start.1 = ((bf16[4,64,8,128]{3,2,0,1:T(8,128)(2,1)}), bf16[4,64,8,128]{3,2,0,1:T(8,128)(2,1)S(1)}, u32[]{:S(2)}, u32[]{:S(2)}) async-start(bf16[4,64,8,128]{3,2,0,1:T(8,128)(2,1)} %copy.42), calls=%async_computation.1 | async-start | bytes 1048576 | tf_op jit(solution)/shard_map/all_to_all | solution.py:91
  68.8 23.4 %all-to-all-start = ((bf16[4,64,8,128]{3,2,0,1:T(8,128)(2,1)}), bf16[4,64,8,128]{3,2,0,1:T(8,128)(2,1)S(1)}, u32[]{:S(2)}, u32[]{:S(2)}) async-start(bf16[4,64,8,128]{3,2,0,1:T(8,128)(2,1)} %copy.40), calls=%async_computation | async-start | bytes 1048576 | tf_op jit(solution)/shard_map/all_to_all | solution.py:90
  74.5 115.8 %all-gather.2.cloned.1.call-start = ((), (), s32[]{:S(2)}) async-start(), calls=%async_computation.4 | async-start | bytes 4259840 | tf_op jit(solution)/shard_map/all_gather | solution.py:124
  94.9 15.1 %collective-permute-start = (bf16[2,4,512,128]{3,2,1,0:T(8,128)(2,1)S(1)}, bf16[2,4,512,128]{3,2,1,0:T(8,128)(2,1)S(1)}, u32[]{:S(2)}, u32[]{:S(2)}) collective-permute-start(bf16[2,4,512,128]{3,2,1,0:T(8,128)(2,1)S(1)} %pad_maximum_fusion.1), channel_id=1, source_target_pairs={{0,8},{8,16},{16,24},{24,32},{32,40},{40,48},{48,56},{56,64},{64,7... | collective-permute-start | bytes 3145736 | tf_op jit(solution)/shard_map/ppermute | solution.py:18
  98.3 16.2 %collective-permute-start.1 = (bf16[2,4,512,128]{3,2,1,0:T(8,128)(2,1)S(1)}, bf16[2,4,512,128]{3,2,1,0:T(8,128)(2,1)}, u32[]{:S(2)}, u32[]{:S(2)}) collective-permute-start(bf16[2,4,512,128]{3,2,1,0:T(8,128)(2,1)S(1)} %pad_maximum_fusion.1), channel_id=1, source_target_pairs={{8,0},{16,8},{24,16},{32,24},{40,32},{48,40},{56,48},{64,56},{72,6... | collective-permute-start | bytes 3145736 | tf_op jit(solution)/shard_map/ppermute | solution.py:20
  100.2 211.7 %all-reduce.3.cloned.1.call-start = ((), (), s32[]{:S(2)}) async-start(), calls=%async_computation.5 | async-start | bytes 8388608 | tf_op jit(solution)/shard_map/psum | solution.py:128
Sparse Core Ops, SparseCore 0:
  100.3 89.9 all-gather.1
  197.0 114.7 all-reduce.2
where the time goes:
time: 322 us; the launch traced here: 321 us
  waiting for transfers between devices  191 us (59%)
  blocking collectives  31.2 us (10%)
  starting transfers between devices  28.6 us (9%)
  local copies, waits for them, and re-layouts  23.8 us (7%)
  matrix products  21.4 us (7%)
  between operations  13.6 us (4%)
  other arithmetic  10.7 us (3%)
    psum x1, waiting for transfers between devices, shards(): lax.psum(partial_value.astype(jnp.bfloat16), 'tp').astype(jnp.float32)  115 us
    all_to_all x1, blocking collectives, shards(): lax.all_to_all(returning, 'seq', split_axis=1, concat_axis=1, tiled=True)  31.2 us
    all_to_all x1, waiting for transfers between devices, shards(): lax.all_to_all(outgoing(2), 'seq', split_axis=1, concat_axis=1, tiled=True)  16.8 us
    all_to_all x1, waiting for transfers between devices, shards(): lax.all_to_all(outgoing(1), 'seq', split_axis=1, concat_axis=1, tiled=True)  16.8 us
    all_to_all x1, waiting for transfers between devices, shards(): lax.all_to_all(outgoing(0), 'seq', split_axis=1, concat_axis=1, tiled=True)  16.1 us
    all_gather x1, waiting for transfers between devices, shards(): lax.all_gather(w_out, 'seq', axis=1, tiled=True)  11.8 us
    all_to_all x1, starting transfers between devices, shards(): lax.all_to_all(outgoing(2), 'seq', split_axis=1, concat_axis=1, tiled=True)  11.6 us
    ppermute x1, waiting for transfers between devices, extended_2(): lax.ppermute(tail, axis, [(i, (i + 1) % count) for i in range(ends)])  9.53 us
  transfers between devices with their start and end apart: 7, of which 7 were waited for; matrix products, arithmetic and copies ran while one was open for 11% of the time, Pallas kernels for 0%

commit v1 on v0

v1 whole, which is shorter than its diff:
```python
import functools

import jax
import jax.numpy as jnp
from jax import lax
from jax.experimental import pallas as pl
from jax.experimental.pallas import tpu as pltpu
from jax.sharding import PartitionSpec as P

MESH = pl.DeviceIdType.MESH
HEAD = 128
CLUSTER = 256
BLOCK = 128
WINDOW = 5 * CLUSTER
LOG2E = 1.4426950408889634


def dot(a, b, contract=((1,), (0,))):
    return lax.dot_general(a, b, (contract, ((), ())), preferred_element_type=jnp.float32)


def attention_kernel(
    peers, planes, heads,
    q_ref, k_ref, v_ref, route_ref, members_ref, pattern_ref,
    gathered,
    index_row, index_col, packed, arrived, query, window, context, leaving, returned,
    send_q, recv_q, send_h, recv_h, send_c, recv_c, send_z, recv_z,
):
    rows = q_ref.shape[0]
    share = rows // peers
    me = lax.axis_index("seq")
    plane = lax.axis_index("tp")
    after, before = lax.rem(me + 1, peers), lax.rem(me + peers - 1, peers)
    above, below = lax.rem(plane + 1, planes), lax.rem(plane + planes - 1, planes)

    barrier = pltpu.get_barrier_semaphore()

    def greet(i, carry):
        pl.semaphore_signal(
            barrier, inc=1, device_id={"seq": lax.rem(me + i, peers)}, device_id_type=MESH
        )
        return carry

    lax.fori_loop(1, peers, greet, 0)
    for other in (above, below):
        pl.semaphore_signal(barrier, inc=1, device_id={"tp": other}, device_id_type=MESH)

    slot = lax.broadcasted_iota(jnp.int32, members_ref.shape, 1)
    order = jnp.concatenate(
        [route_ref[...], lax.div(members_ref[...], rows) * rows + slot], axis=0
    ).astype(jnp.float32)
    order_col = order.T
    ranks = []
    for i in range(2 * heads):
        smaller = order_col[:, i : i + 1] < order[i : i + 1, :]
        ranks.append(jnp.sum(smaller.astype(jnp.float32), axis=0, keepdims=True))
    ranks = jnp.concatenate(ranks, axis=0)
    index_row[...] = ranks.astype(jnp.int32)
    index_col[...] = ranks.T.astype(jnp.int32)

    def table(i):
        at = lax.broadcasted_iota(jnp.int32, (rows, rows), 0)
        return (at == index_row[i : i + 1, :]).astype(jnp.bfloat16)

    def table_t(i):
        at = lax.broadcasted_iota(jnp.int32, (rows, rows), 1)
        return (at == index_col[:, i : i + 1]).astype(jnp.bfloat16)

    def to_all(source, landing, send_sem, recv_sem, h):
        def send(i, carry):
            peer = lax.rem(me + i, peers)
            pltpu.make_async_remote_copy(
                src_ref=source.at[h, peer], dst_ref=landing.at[h, me],
                send_sem=send_sem.at[h], recv_sem=recv_sem.at[h],
                device_id={"seq": peer}, device_id_type=MESH,
            ).start()
            return carry

        lax.fori_loop(1, peers, send, 0)
        landing[h, me] = source[h, me]

    def all_of(source, landing, send_sem, recv_sem, h):
        others = pl.ds(0, peers - 1)
        return pltpu.make_async_remote_copy(
            src_ref=source.at[h, others], dst_ref=landing.at[h, others],
            send_sem=send_sem.at[h], recv_sem=recv_sem.at[h],
            device_id={"seq": after}, device_id_type=MESH,
        )

    def halo(h, side):
        own = window.at[h, pl.ds(rows, rows)]
        landing = window.at[h, pl.ds(0 if side == 0 else 2 * rows, rows)]
        return pltpu.make_async_remote_copy(
            src_ref=own, dst_ref=landing,
            send_sem=send_h.at[h, side], recv_sem=recv_h.at[h, side],
            device_id={"seq": after if side == 0 else before}, device_id_type=MESH,
        )

    def hops(h, way):
        return planes // 2 - (h + way) % 2

    def ring(h, way, hop):
        held = lax.rem(plane + planes - hop if way == 0 else plane + hop, planes)
        block = gathered.at[held, h]
        return pltpu.make_async_remote_copy(
            src_ref=block, dst_ref=block,
            send_sem=send_z.at[h, way, hop], recv_sem=recv_z.at[h, way, hop],
            device_id={"tp": above if way == 0 else below}, device_id_type=MESH,
        )

    def send_qkv(h):
        columns = slice(h * HEAD, (h + 1) * HEAD)
        stacked = jnp.concatenate([q_ref[:, columns], k_ref[:, columns], v_ref[:, columns]], axis=1)
        packed[h] = dot(table(h), stacked).reshape(peers, share, 3 * HEAD).astype(jnp.bfloat16)

    def start_qkv(h):
        to_all(packed, arrived, send_q, recv_q, h)

    def land(h):
        all_of(packed, arrived, send_q, recv_q, h).wait_recv()
        came = arrived[h].astype(jnp.float32).reshape(rows, 3 * HEAD).astype(jnp.bfloat16)
        placed = dot(table_t(heads + h), came).astype(jnp.bfloat16)
        query[h] = placed[:, :HEAD]
        window[h, pl.ds(rows, rows)] = placed[:, HEAD:]
        halo(h, 0).start()
        halo(h, 1).start()

    def attend(h):
        halo(h, 0).wait_recv()
        halo(h, 1).wait_recv()

        def cluster(c, carry):
            start = pl.multiple_of(c * CLUSTER, CLUSTER)
            q = query[h, pl.ds(start, CLUSTER)]
            kv = window.at[h, pl.ds(start, WINDOW)]
            scores = dot(q, kv[:, :HEAD], ((1,), (1,))) * (HEAD**-0.5 * LOG2E)
            parts = []
            for b in range(WINDOW // BLOCK):
                bias = jnp.where(pattern_ref[h, c, b] > 0, 0.0, -jnp.inf)
                parts.append(scores[:, b * BLOCK : (b + 1) * BLOCK] + bias)
            scores = jnp.concatenate(parts, axis=1)
            top = jnp.max(scores, axis=1, keepdims=True)
            weights = jnp.exp2(scores - top)
            total = jnp.sum(weights, axis=1, keepdims=True)
            mixed = dot(weights.astype(jnp.bfloat16), kv[:, HEAD:])
            context[pl.ds(start, CLUSTER)] = (mixed / total).astype(jnp.bfloat16)
            return carry

        lax.fori_loop(0, rows // CLUSTER, cluster, 0)
        back = dot(table(heads + h), context[...])
        leaving[h] = back.reshape(peers, share, HEAD).astype(jnp.bfloat16)
        to_all(leaving, returned, send_c, recv_c, h)

    def collect(h):
        all_of(leaving, returned, send_c, recv_c, h).wait_recv()
        came = returned[h].astype(jnp.float32).reshape(rows, HEAD).astype(jnp.bfloat16)
        gathered[plane, h] = dot(table_t(h), came).astype(jnp.bfloat16)
        ring(h, 0, 0).start()
        ring(h, 1, 0).start()

    def forward(h, hop):
        for way in (0, 1):
            if hop <= hops(h, way):
                ring(h, way, hop - 1).wait_recv()
                if hop < hops(h, way):
                    ring(h, way, hop).start()

    send_qkv(0)
    pl.semaphore_wait(barrier, peers + 1)
    start_qkv(0)
    send_qkv(1)
    start_qkv(1)
    land(0)
    send_qkv(2)
    start_qkv(2)
    attend(0)
    land(1)
    send_qkv(3)
    start_qkv(3)
    attend(1)
    collect(0)
    land(2)
    forward(0, 1)
    attend(2)
    forward(0, 2)
    collect(1)
    forward(0, 3)
    forward(1, 1)
    land(3)
    forward(0, 4)
    forward(1, 2)
    attend(3)
    collect(2)
    forward(1, 3)
    forward(2, 1)
    collect(3)
    forward(1, 4)
    forward(2, 2)
    forward(3, 1)
    forward(2, 3)
    forward(3, 2)
    forward(2, 4)
    forward(3, 3)
    forward(3, 4)

    for h in range(heads):
        all_of(packed, arrived, send_q, recv_q, h).wait_send()
        all_of(leaving, returned, send_c, recv_c, h).wait_send()
        for side in (0, 1):
            halo(h, side).wait_send()
        for way in (0, 1):
            for hop in range(hops(h, way)):
                ring(h, way, hop).wait_send()


def project_kernel(heads, a_ref, w_ref, o_ref, total):
    step = pl.program_id(0)
    here = jnp.concatenate([a_ref[0, h] for h in range(heads)], axis=1)
    part = dot(here, w_ref[...], ((1,), (1,)))

    @pl.when(step == 0)
    def _():
        total[...] = part

    @pl.when(step > 0)
    def _():
        total[...] += part

    @pl.when(step == pl.num_programs(0) - 1)
    def _():
        o_ref[...] = total[...].astype(o_ref.dtype)


def shards(queries, keys, values, route, members, pattern, w_out):
    rows = queries.shape[0]
    heads = route.shape[0]
    peers, planes = lax.axis_size("seq"), lax.axis_size("tp")
    share = rows // peers
    bf16 = jnp.bfloat16

    inner = peers // planes
    swap = []
    for y in range(planes):
        for i in range(inner):
            for z in range(planes):
                swap.append(((y * inner + i) * planes + z, (z * inner + i) * planes + y))
    turned = lax.ppermute(w_out.T, ("seq", "tp"), swap)
    weights = lax.all_gather(turned, "seq", axis=0, tiled=True)

    whole = pl.BlockSpec(memory_space=pltpu.VMEM)
    gathered = pl.pallas_call(
        functools.partial(attention_kernel, peers, planes, heads),
        out_shape=jax.ShapeDtypeStruct((planes, heads, rows, HEAD), bf16),
        in_specs=[whole] * 5 + [pl.BlockSpec(memory_space=pltpu.SMEM)],
        out_specs=whole,
        scratch_shapes=[
            pltpu.VMEM((2 * heads, rows), jnp.int32),
            pltpu.VMEM((rows, 2 * heads), jnp.int32),
            pltpu.VMEM((heads, peers, share, 3 * HEAD), bf16),
            pltpu.VMEM((heads, peers, share, 3 * HEAD), bf16),
            pltpu.VMEM((heads, rows, HEAD), bf16),
            pltpu.VMEM((heads, 3 * rows, 2 * HEAD), bf16),
            pltpu.VMEM((rows, HEAD), bf16),
            pltpu.VMEM((heads, peers, share, HEAD), bf16),
            pltpu.VMEM((heads, peers, share, HEAD), bf16),
            pltpu.SemaphoreType.DMA((heads,)),
            pltpu.SemaphoreType.DMA((heads,)),
            pltpu.SemaphoreType.DMA((heads, 2)),
            pltpu.SemaphoreType.DMA((heads, 2)),
            pltpu.SemaphoreType.DMA((heads,)),
            pltpu.SemaphoreType.DMA((heads,)),
            pltpu.SemaphoreType.DMA((heads, 2, planes // 2)),
            pltpu.SemaphoreType.DMA((heads, 2, planes // 2)),
        ],
        compiler_params=pltpu.CompilerParams(
            collective_id=0, has_side_effects=True, vmem_limit_bytes=48 * 2**20
        ),
        cost_estimate=pl.CostEstimate(
            flops=4 * 10**9, bytes_accessed=6 * 2**20, transcendentals=3 * 10**6
        ),
    )(queries, keys, values, route, members, pattern)

    return pl.pallas_call(
        functools.partial(project_kernel, heads),
        grid=(planes,),
        out_shape=jax.ShapeDtypeStruct((rows, rows), bf16),
        in_specs=[
            pl.BlockSpec((1, heads, rows, HEAD), lambda g: (g, 0, 0, 0)),
            pl.BlockSpec((rows, heads * HEAD), lambda g: (g, 0)),
        ],
        out_specs=pl.BlockSpec((rows, rows), lambda g: (0, 0)),
        scratch_shapes=[pltpu.VMEM((rows, rows), jnp.float32)],
        compiler_params=pltpu.CompilerParams(vmem_limit_bytes=16 * 2**20),
    )(gathered, weights)


def solution(mesh):
    placed = (
        P("seq", "tp"),
        P("seq", "tp"),
        P("seq", "tp"),
        P("tp", "seq"),
        P("tp", "seq"),
        P("tp", "seq", None),
        P("tp", "seq"),
    )
    return jax.shard_map(
        shards, mesh=mesh, in_specs=placed, out_specs=P("seq", "tp"), check_vma=False
    )
```

time: 322 us -> 169 us (0.52)
  waiting for transfers between devices: 191 us -> 0.02 us
  Pallas kernels: 0 us -> 142 us
  blocking collectives: 31.2 us -> 0 us
  starting transfers between devices: 28.6 us -> 1.49 us
  matrix products: 21.4 us -> 0 us
  local copies, waits for them, and re-layouts: 23.8 us -> 12.2 us
  other arithmetic: 10.7 us -> 0 us
    pallas_call x0 -> x2, Pallas kernels: none -> 142 us  [the longest x1 136 us: shards(): pl.pallas_call(functools.partial(attention_kernel, peers, planes, heads),...]
    psum x1 -> x0, waiting for transfers between devices: 115 us -> none  [shards(): lax.psum(partial_value.astype(jnp.bfloat16), 'tp').astype(jnp.float32)]
    all_to_all x3 -> x0, waiting for transfers between devices: 49.8 us -> none  [the longest x1 16.8 us: shards(): lax.all_to_all(outgoing(2), 'seq', split_axis=1, concat_axis=1, tiled=True)]
    all_to_all x1 -> x0, blocking collectives: 31.2 us -> none  [shards(): lax.all_to_all(returning, 'seq', split_axis=1, concat_axis=1, tiled=True)]
    all_to_all x3 -> x0, starting transfers between devices: 23.1 us -> none  [the longest x1 11.6 us: shards(): lax.all_to_all(outgoing(2), 'seq', split_axis=1, concat_axis=1, tiled=True)]
    dot_general x9 -> x0, matrix products: 17.5 us -> none  [the longest x1 6.57 us: shards(): jnp.dot(attended, lax.all_gather(w_out, 'seq', axis=1, tiled=True), prefe...]
    ppermute x2 -> x1, waiting for transfers between devices: 14 us -> 0.01 us  [shards(): turned = lax.ppermute(w_out.T, ('seq', 'tp'), swap)]
    all_gather x1, waiting for transfers between devices: 11.8 us -> 0.01 us  [shards(): weights = lax.all_gather(turned, 'seq', axis=0, tiled=True)]
  transfers between devices with their start and end apart: 7 -> 2, of which waited for: 7 -> 0; matrix products, arithmetic and copies ran while one was open for 11% -> 0% of each run, Pallas kernels for 0% -> 81%
where the time goes in v1:
time: 169 us
  Pallas kernels  142 us (84%)
  between operations  13.4 us (8%)
  local copies, waits for them, and re-layouts  12.2 us (7%)
    pallas_call x1, Pallas kernels, shards(): pl.pallas_call(functools.partial(attention_kernel, peers, planes, heads),...  136 us
    unnamed x20, local copies, waits for them, and re-layouts  12.2 us
    pallas_call x1, Pallas kernels, shards(): pl.pallas_call(functools.partial(project_kernel, heads), grid=(planes,),...  5.43 us
  transfers between devices with their start and end apart: 2, of which 0 were waited for; matrix products, arithmetic and copies ran while one was open for 0% of the time, Pallas kernels for 81%

profile of v1, /device:TPU:1, one launch (start us, length us, event | category | flops | bytes accessed | tf_op | source)
XLA Modules:
  0.0 168.7 jit_solution(16934537150325636342)
XLA Ops:
  6.5 0.0 all-gather.2.cloned.1.call-start
  6.5 1.5 collective-permute-start
  8.0 0.0 collective-permute-done
  8.0 0.0 copy-start.9
  8.0 0.6 copy-done.9
  8.7 0.0 all-gather.2.cloned.1.call-update
  8.7 0.0 copy-start.3
  8.7 1.0 copy-done.3
  9.7 0.0 copy-start.4
  9.7 1.0 copy-done.4
  10.8 0.0 copy-start.5
  10.8 1.0 copy-done.5
  11.8 0.0 copy-start.6
  11.8 0.7 copy-done.6
  12.5 0.0 copy-start.7
  12.5 0.7 copy-done.7
  13.2 0.0 copy-start.8
  13.2 0.7 copy-done.8
  13.9 136.2 %shard_map.73.a_ref = bf16[8,4,512,128]{3,2,1,0:T(8,128)(2,1)S(1)} custom-call(bf16[512,512]{1,0:T(8,128)(2,1)S(1)} %copy-done.3, bf16[512,512]{1,0:T(8,128)(2,1)S(1)} %copy-done.4, bf16[512,512]{1,0:T(8,128)(2,1)S(1)} %copy-done.5, s32[4,512]{1,0:T(4,128)S(1)} %copy-done.6, s32[4,512]{1,0:T(4,128)S(1)} %copy-done.7, s32[4,2,10]{2,1,0:T(2,128)S(1)} %copy-done.8), custom_call_target="tpu_custom_call" | custom-call | flops 4000000000 | bytes 6291456 | tf_op jit(solution)/shard_map/pallas_call | solution.py:251
  150.1 0.0 copy-start.1
  150.1 2.0 %copy-done.1 = bf16[8,4,512,128]{3,2,1,0:T(8,128)(2,1)} copy-done((bf16[8,4,512,128]{3,2,1,0:T(8,128)(2,1)}, bf16[8,4,512,128]{3,2,1,0:T(8,128)(2,1)S(1)}, u32[]{:S(2)}) %copy-start.1) | copy-done | bytes 4194328
  152.0 0.0 all-gather.2.cloned.1.call-done.w_ref
  152.1 0.0 copy-start
  152.1 2.2 %copy-done = bf16[4096,512]{1,0:T(8,128)(2,1)S(1)} copy-done((bf16[4096,512]{1,0:T(8,128)(2,1)S(1)}, bf16[4096,512]{1,0:T(8,128)(2,1)}, u32[]{:S(2)}) %copy-start) | copy-done | bytes 4194328
  154.2 0.0 copy-start.2
  154.2 2.2 %copy-done.2 = bf16[8,4,512,128]{3,2,1,0:T(8,128)(2,1)S(1)} copy-done((bf16[8,4,512,128]{3,2,1,0:T(8,128)(2,1)S(1)}, bf16[8,4,512,128]{3,2,1,0:T(8,128)(2,1)}, u32[]{:S(2)}) %copy-start.2) | copy-done | bytes 4194328
  156.4 5.4 %shard_map.74 = bf16[512,512]{1,0:T(8,128)(2,1)} custom-call(bf16[8,4,512,128]{3,2,1,0:T(8,128)(2,1)S(1)} %copy-done.2, bf16[4096,512]{1,0:T(8,128)(2,1)S(1)} %copy-done), custom_call_target="tpu_custom_call" | custom-call | tf_op jit(solution)/shard_map/pallas_call | solution.py:283
Async XLA Ops:
  6.5 145.5 %all-gather.2.cloned.1.call-start = ((), (), s32[]{:S(2)}) async-start(), calls=%async_computation | async-start | bytes 4259840 | tf_op jit(solution)/shard_map/all_gather | solution.py:248
  6.5 1.5 collective-permute-start
  8.0 0.6 copy-start.9
  8.7 1.0 copy-start.3
  9.7 1.0 copy-start.4
  10.8 1.0 copy-start.5
  11.8 0.7 copy-start.6
  12.5 0.7 copy-start.7
  13.2 0.7 copy-start.8
  150.1 2.0 %copy-start.1 = (bf16[8,4,512,128]{3,2,1,0:T(8,128)(2,1)}, bf16[8,4,512,128]{3,2,1,0:T(8,128)(2,1)S(1)}, u32[]{:S(2)}) copy-start(bf16[8,4,512,128]{3,2,1,0:T(8,128)(2,1)S(1)} %shard_map.73.a_ref) | copy-start | bytes 12582916
  152.1 2.2 %copy-start = (bf16[4096,512]{1,0:T(8,128)(2,1)S(1)}, bf16[4096,512]{1,0:T(8,128)(2,1)}, u32[]{:S(2)}) copy-start(bf16[4096,512]{1,0:T(8,128)(2,1)} %all-gather.2.cloned.1.call-done.w_ref) | copy-start | bytes 12582916
  154.2 2.2 %copy-start.2 = (bf16[8,4,512,128]{3,2,1,0:T(8,128)(2,1)S(1)}, bf16[8,4,512,128]{3,2,1,0:T(8,128)(2,1)}, u32[]{:S(2)}) copy-start(bf16[8,4,512,128]{3,2,1,0:T(8,128)(2,1)} %copy-done.1) | copy-start | bytes 12582916
Sparse Core Ops, SparseCore 0:
  10.7 108.4 all-gather.1

commit v2 on v1

v2 whole, which is shorter than its diff:
```python
import functools

import jax
import jax.numpy as jnp
from jax import lax
from jax.experimental import pallas as pl
from jax.experimental.pallas import tpu as pltpu
from jax.sharding import PartitionSpec as P

MESH = pl.DeviceIdType.MESH
HEAD = 128
CLUSTER = 256
BLOCK = 128
WINDOW = 5 * CLUSTER
LOG2E = 1.4426950408889634


def dot(a, b, contract=((1,), (0,))):
    return lax.dot_general(a, b, (contract, ((), ())), preferred_element_type=jnp.float32)


def layer_kernel(
    peers, planes, heads,
    q_hbm, k_hbm, v_hbm, route_hbm, members_hbm, pattern_hbm, w_hbm,
    mixed,
    q_ref, k_ref, v_ref, route_ref, members_ref, pattern_ref,
    index_row, index_col, packed, arrived, query, window, context, leaving, returned,
    gathered, weights, total,
    load, send_q, recv_q, send_h, recv_h, send_c, recv_c, send_z, recv_z, send_w, recv_w,
):
    rows = q_ref.shape[0]
    share = rows // peers
    inner = peers // planes
    me = lax.axis_index("seq")
    plane = lax.axis_index("tp")
    after, before = me + 1, me - 1
    above, below = lax.rem(plane + 1, planes), lax.rem(plane + planes - 1, planes)
    line, place = lax.div(me, inner), lax.rem(me, inner)
    column, core = lax.div(place, 2), lax.rem(place, 2)
    columns = inner // 2
    sibling = me + 1 - 2 * core
    has_before, has_after = me > 0, me < peers - 1
    turned = line != plane

    loads = [
        pltpu.make_async_copy(source, target, load.at[i])
        for i, (source, target) in enumerate(
            (
                (route_hbm, route_ref),
                (members_hbm, members_ref),
                (q_hbm, q_ref),
                (k_hbm, k_ref),
                (v_hbm, v_ref),
                (pattern_hbm, pattern_ref),
            )
        )
    ]
    for copy in loads:
        copy.start()

    barrier = pltpu.get_barrier_semaphore()

    def greet(i, carry):
        pl.semaphore_signal(
            barrier, inc=1, device_id={"seq": lax.rem(me + i, peers)}, device_id_type=MESH
        )
        return carry

    lax.fori_loop(1, peers, greet, 0)
    for other in (above, below):
        pl.semaphore_signal(barrier, inc=1, device_id={"tp": other}, device_id_type=MESH)

    mirror = {"seq": plane * inner + place, "tp": line}

    @pl.when(turned)
    def _():
        pl.semaphore_signal(barrier, inc=1, device_id=mirror, device_id_type=MESH)

    def meet():
        @pl.when(turned)
        def _():
            pl.semaphore_wait(barrier, peers + 2)

        @pl.when(jnp.logical_not(turned))
        def _():
            pl.semaphore_wait(barrier, peers + 1)

    def rank(i, order, order_col):
        smaller = order_col[:, i : i + 1] < order[i : i + 1, :]
        return jnp.sum(smaller.astype(jnp.float32), axis=0, keepdims=True)

    def table(i):
        at = lax.broadcasted_iota(jnp.int32, (rows, rows), 0)
        return (at == index_row[i : i + 1, :]).astype(jnp.bfloat16)

    def table_t(i):
        at = lax.broadcasted_iota(jnp.int32, (rows, rows), 1)
        return (at == index_col[:, i : i + 1]).astype(jnp.bfloat16)

    def to_all(source, landing, send_sem, recv_sem, h):
        def send(i, carry):
            peer = lax.rem(me + i, peers)
            pltpu.make_async_remote_copy(
                src_ref=source.at[h, peer], dst_ref=landing.at[h, me],
                send_sem=send_sem.at[h], recv_sem=recv_sem.at[h],
                device_id={"seq": peer}, device_id_type=MESH,
            ).start()
            return carry

        lax.fori_loop(1, peers, send, 0)
        landing[h, me] = source[h, me]

    def all_of(source, landing, send_sem, recv_sem, h):
        others = pl.ds(0, peers - 1)
        return pltpu.make_async_remote_copy(
            src_ref=source.at[h, others], dst_ref=landing.at[h, others],
            send_sem=send_sem.at[h], recv_sem=recv_sem.at[h],
            device_id={"seq": sibling}, device_id_type=MESH,
        )

    def halo(h, side):
        own = window.at[h, pl.ds(rows, rows)]
        landing = window.at[h, pl.ds(0 if side == 0 else 2 * rows, rows)]
        return pltpu.make_async_remote_copy(
            src_ref=own, dst_ref=landing,
            send_sem=send_h.at[h, side], recv_sem=recv_h.at[h, side],
            device_id={"seq": after if side == 0 else before}, device_id_type=MESH,
        )

    def hops(h, way):
        return planes // 2 - (h + way) % 2

    def ring(h, way, hop):
        held = lax.rem(plane + planes - hop if way == 0 else plane + hop, planes)
        block = gathered.at[held, h]
        return pltpu.make_async_remote_copy(
            src_ref=block, dst_ref=block,
            send_sem=send_z.at[h, way, hop], recv_sem=recv_z.at[h, way, hop],
            device_id={"tp": above if way == 0 else below}, device_id_type=MESH,
        )

    def w_copy(i, block, to):
        return pltpu.make_async_remote_copy(
            src_ref=block, dst_ref=block, send_sem=send_w.at[i], recv_sem=recv_w.at[i],
            device_id={"seq": to}, device_id_type=MESH,
        )

    def w_turn():
        return pltpu.make_async_remote_copy(
            src_ref=w_hbm, dst_ref=weights.at[plane, place],
            send_sem=send_w.at[0], recv_sem=recv_w.at[0],
            device_id=mirror, device_id_type=MESH,
        )

    def w_line(way, hop):
        held = lax.rem(line + planes - hop if way == 0 else line + hop, planes)
        to = lax.rem(line + (1 if way == 0 else planes - 1), planes)
        return w_copy(1 + way * 4 + hop, weights.at[held, place], to * inner + place)

    def beside(step):
        return lax.rem(column + columns + step, columns)

    def w_near(way):
        to = beside(1 if way == 0 else -1)
        return w_copy(9 + way, weights.at[:, place], line * inner + to * 2 + core)

    def w_far(way):
        to, held = (beside(1), beside(-1)) if way == 0 else (beside(-1), beside(1))
        half = pl.ds(way * (planes // 2), planes // 2)
        return w_copy(11 + way, weights.at[half, held * 2 + core], line * inner + to * 2 + core)

    def w_pair(step):
        return w_copy(13 + step, weights.at[:, beside(step) * 2 + core], sibling)

    def w_begin():
        @pl.when(turned)
        def _():
            w_turn().start()

        @pl.when(jnp.logical_not(turned))
        def _():
            pltpu.make_async_copy(w_hbm, weights.at[plane, place], recv_w.at[0]).start()

    def w_step(hop):
        if hop == 0:
            w_turn().wait_recv()
        for way in (0, 1):
            if 0 < hop <= 4 - way:
                w_line(way, hop - 1).wait_recv()
            if hop < 4 - way:
                w_line(way, hop).start()
        if hop == 4:
            w_near(0).start()
            w_near(1).start()
            w_pair(0).start()
        if hop == 5:
            w_near(0).wait_recv()
            w_near(1).wait_recv()
            w_far(0).start()
            w_far(1).start()
            w_pair(1).start()
            w_pair(3).start()
        if hop == 6:
            w_far(0).wait_recv()
            w_far(1).wait_recv()
            w_pair(2).start()
        if hop == 7:
            for step in range(columns):
                w_pair(step).wait_recv()

    def pack(h):
        at = slice(h * HEAD, (h + 1) * HEAD)
        stacked = jnp.concatenate([q_ref[:, at], k_ref[:, at], v_ref[:, at]], axis=1)
        packed[h] = dot(table(h), stacked).reshape(peers, share, 3 * HEAD).astype(jnp.bfloat16)

    def send(h):
        to_all(packed, arrived, send_q, recv_q, h)

    def land(h):
        all_of(packed, arrived, send_q, recv_q, h).wait_recv()
        came = arrived[h].astype(jnp.float32).reshape(rows, 3 * HEAD).astype(jnp.bfloat16)
        placed = dot(table_t(heads + h), came).astype(jnp.bfloat16)
        window[h, pl.ds(rows, rows)] = placed[:, HEAD:]

        @pl.when(has_after)
        def _():
            halo(h, 0).start()

        @pl.when(has_before)
        def _():
            halo(h, 1).start()

        query[h] = placed[:, :HEAD]

    def attend(h):
        @pl.when(has_before)
        def _():
            halo(h, 0).wait_recv()

        @pl.when(has_after)
        def _():
            halo(h, 1).wait_recv()

        def cluster(c, carry):
            start = pl.multiple_of(c * CLUSTER, CLUSTER)
            q = query[h, pl.ds(start, CLUSTER)]
            kv = window.at[h, pl.ds(start, WINDOW)]
            scores = dot(q, kv[:, :HEAD], ((1,), (1,))) * (HEAD**-0.5 * LOG2E)
            parts = []
            for b in range(WINDOW // BLOCK):
                bias = jnp.where(pattern_ref[h, c, b] > 0, 0.0, -jnp.inf)
                parts.append(scores[:, b * BLOCK : (b + 1) * BLOCK] + bias)
            scores = jnp.concatenate(parts, axis=1)
            top = jnp.max(scores, axis=1, keepdims=True)
            chances = jnp.exp2(scores - top)
            mass = jnp.sum(chances, axis=1, keepdims=True)
            summed = dot(chances.astype(jnp.bfloat16), kv[:, HEAD:])
            context[pl.ds(start, CLUSTER)] = (summed / mass).astype(jnp.bfloat16)
            return carry

        lax.fori_loop(0, rows // CLUSTER, cluster, 0)
        back = dot(table(heads + h), context[...])
        leaving[h] = back.reshape(peers, share, HEAD).astype(jnp.bfloat16)
        to_all(leaving, returned, send_c, recv_c, h)

    def collect(h):
        all_of(leaving, returned, send_c, recv_c, h).wait_recv()
        came = returned[h].astype(jnp.float32).reshape(rows, HEAD).astype(jnp.bfloat16)
        gathered[plane, h] = dot(table_t(h), came).astype(jnp.bfloat16)
        ring(h, 0, 0).start()
        ring(h, 1, 0).start()

    def forward(h, hop):
        for way in (0, 1):
            if hop <= hops(h, way):
                ring(h, way, hop - 1).wait_recv()
                if hop < hops(h, way):
                    ring(h, way, hop).start()

    def project(group, first):
        held = lax.rem(plane + group, planes)
        here = jnp.concatenate([gathered[held, first], gathered[held, first + 1]], axis=1)
        block = weights[held, :, :, first * HEAD : (first + 2) * HEAD].reshape(rows, 2 * HEAD)
        return dot(here, block, ((1,), (1,)))

    loads[0].wait()
    loads[1].wait()
    slot = lax.broadcasted_iota(jnp.int32, members_ref.shape, 1)
    order = jnp.concatenate(
        [route_ref[...], lax.div(members_ref[...], rows) * rows + slot], axis=0
    ).astype(jnp.float32)
    order_col = order.T
    ranks = [rank(0, order, order_col)]
    index_row[0:1, :] = ranks[0].astype(jnp.int32)
    for copy in loads[2:]:
        copy.wait()
    pack(0)
    meet()
    send(0)
    for i in range(1, 2 * heads):
        ranks.append(rank(i, order, order_col))
        index_row[i : i + 1, :] = ranks[i].astype(jnp.int32)
        if i == 1:
            pack(1)
            send(1)
    index_col[...] = jnp.concatenate(ranks, axis=0).T.astype(jnp.int32)

    @pl.when(jnp.logical_not(has_before))
    def _():
        for h in range(heads):
            window[h, pl.ds(0, rows)] = jnp.zeros((rows, 2 * HEAD), jnp.bfloat16)

    @pl.when(jnp.logical_not(has_after))
    def _():
        for h in range(heads):
            window[h, pl.ds(2 * rows, rows)] = jnp.zeros((rows, 2 * HEAD), jnp.bfloat16)

    land(0)
    pack(2)
    send(2)
    w_begin()
    attend(0)
    land(1)
    pack(3)
    send(3)
    w_step(0)
    attend(1)
    collect(0)
    w_step(1)
    land(2)
    forward(0, 1)
    w_step(2)
    attend(2)
    collect(1)
    forward(0, 2)
    w_step(3)
    land(3)
    forward(0, 3)
    forward(1, 1)
    w_step(4)
    attend(3)
    collect(2)
    forward(1, 2)
    forward(0, 4)
    w_step(5)
    forward(2, 1)
    forward(1, 3)
    collect(3)
    forward(2, 2)
    forward(3, 1)
    w_step(6)
    forward(1, 4)
    forward(2, 3)
    forward(3, 2)
    w_step(7)
    total[...] = project(0, 0)
    def add(group, carry):
        total[...] += project(group, 0)
        return carry

    forward(2, 4)
    lax.fori_loop(1, planes, add, 0)
    total[...] += project(0, 2)
    for hop in (1, 2):
        total[...] += project(planes - hop, 2)
        total[...] += project(hop, 2)
    forward(3, 3)
    total[...] += project(planes - 3, 2)
    total[...] += project(3, 2)
    forward(3, 4)
    total[...] += project(4, 2)

    for h in range(heads):
        all_of(packed, arrived, send_q, recv_q, h).wait_send()
        all_of(leaving, returned, send_c, recv_c, h).wait_send()

        @pl.when(has_after)
        def _():
            halo(h, 0).wait_send()

        @pl.when(has_before)
        def _():
            halo(h, 1).wait_send()

        for way in (0, 1):
            for hop in range(hops(h, way)):
                ring(h, way, hop).wait_send()

    @pl.when(turned)
    def _():
        w_turn().wait_send()

    for way in (0, 1):
        for hop in range(4 - way):
            w_line(way, hop).wait_send()
        w_near(way).wait_send()
        w_far(way).wait_send()
    for step in range(columns):
        w_pair(step).wait_send()
    mixed[...] = total[...].astype(mixed.dtype)


def shards(queries, keys, values, route, members, pattern, w_out):
    rows = queries.shape[0]
    heads = route.shape[0]
    peers, planes = lax.axis_size("seq"), lax.axis_size("tp")
    share, inner = rows // peers, peers // planes
    bf16 = jnp.bfloat16
    vmem, dma = pltpu.VMEM, pltpu.SemaphoreType.DMA
    return pl.pallas_call(
        functools.partial(layer_kernel, peers, planes, heads),
        out_shape=jax.ShapeDtypeStruct((rows, rows), bf16),
        in_specs=[pl.BlockSpec(memory_space=pltpu.HBM)] * 7,
        out_specs=pl.BlockSpec(memory_space=pltpu.VMEM),
        scratch_shapes=[
            vmem(queries.shape, bf16),
            vmem(keys.shape, bf16),
            vmem(values.shape, bf16),
            vmem(route.shape, jnp.int32),
            vmem(members.shape, jnp.int32),
            pltpu.SMEM(pattern.shape, jnp.int32),
            vmem((2 * heads, rows), jnp.int32),
            vmem((rows, 2 * heads), jnp.int32),
            vmem((heads, peers, share, 3 * HEAD), bf16),
            vmem((heads, peers, share, 3 * HEAD), bf16),
            vmem((heads, rows, HEAD), bf16),
            vmem((heads, 3 * rows, 2 * HEAD), bf16),
            vmem((rows, HEAD), bf16),
            vmem((heads, peers, share, HEAD), bf16),
            vmem((heads, peers, share, HEAD), bf16),
            vmem((planes, heads, rows, HEAD), bf16),
            vmem((planes, inner, rows // inner, heads * HEAD), bf16),
            vmem((rows, rows), jnp.float32),
            dma((6,)),
            dma((heads,)),
            dma((heads,)),
            dma((heads, 2)),
            dma((heads, 2)),
            dma((heads,)),
            dma((heads,)),
            dma((heads, 2, planes // 2)),
            dma((heads, 2, planes // 2)),
            dma((17,)),
            dma((17,)),
        ],
        compiler_params=pltpu.CompilerParams(
            collective_id=0, has_side_effects=True, vmem_limit_bytes=56 * 2**20
        ),
        cost_estimate=pl.CostEstimate(
            flops=7 * 10**9, bytes_accessed=3 * 2**20, transcendentals=3 * 10**6
        ),
    )(queries, keys, values, route, members, pattern, w_out.T)


def solution(mesh):
    placed = (
        P("seq", "tp"),
        P("seq", "tp"),
        P("seq", "tp"),
        P("tp", "seq"),
        P("tp", "seq"),
        P("tp", "seq", None),
        P("tp", "seq"),
    )
    return jax.shard_map(
        shards, mesh=mesh, in_specs=placed, out_specs=P("seq", "tp"), check_vma=False
    )
```

time: 169 us -> 126 us (0.75)
  Pallas kernels: 142 us -> 123 us
  between operations: 13.4 us -> 0.01 us
  local copies, waits for them, and re-layouts: 12.2 us -> 1.87 us
    pallas_call x2 -> x1, Pallas kernels: 142 us -> 123 us  [shards(): pl.pallas_call(functools.partial(layer_kernel, peers, planes, heads), out...]
    unnamed x20 -> x1, local copies, waits for them, and re-layouts: 12.2 us -> 1.87 us
  transfers between devices with their start and end apart: 2 -> 0, of which waited for: 0 -> 0; matrix products, arithmetic and copies ran while one was open for 0% -> 0% of each run, Pallas kernels for 81% -> 0%
where the time goes in v2:
time: 126 us; the launch traced here: 125 us
  Pallas kernels  123 us (98%)
  local copies, waits for them, and re-layouts  1.87 us (1%)
    pallas_call x1, Pallas kernels, shards(): pl.pallas_call(functools.partial(layer_kernel, peers, planes, heads), out...  123 us

profile of v2, /device:TPU:1, one launch (start us, length us, event | category | flops | bytes accessed | tf_op | source)
XLA Modules:
  0.0 124.9 jit_solution(13350637680542895174)
XLA Ops:
  0.0 123.1 %shard_map.73 = bf16[512,512]{1,0:T(8,128)(2,1)} custom-call(bf16[512,512]{1,0:T(8,128)(2,1)} %q_hbm.1, bf16[512,512]{1,0:T(8,128)(2,1)} %k_hbm.1, bf16[512,512]{1,0:T(8,128)(2,1)} %v_hbm.1, s32[4,512]{1,0:T(4,128)} %route_hbm.1, s32[4,512]{1,0:T(4,128)} %members_hbm.1, s32[4,2,10]{2,1,0:T(2,128)} %pattern_hbm.1, bf16[64,512]{1,0:T(8,128)(2,1)} %bitcast.1), custom_call_target="tpu_custom_call" | custom-call | flops 7000000000 | bytes 3145728 | tf_op jit(solution)/shard_map/pallas_call | solution.py:410
  123.1 1.9 %copy.9 = bf16[512,512]{1,0:T(8,128)(2,1)} copy(bf16[512,512]{1,0:T(8,128)(2,1)} %shard_map.73) | data formatting | bytes 1048576

commit v3 on v2

--- a/solution.py
+++ b/solution.py
@@ -353,20 +353,20 @@
     forward(2, 3)
     forward(3, 2)
     w_step(7)
-    total[...] = project(0, 0)
+    forward(2, 4)
+
     def add(group, carry):
         total[...] += project(group, 0)
         return carry
 
-    forward(2, 4)
-    lax.fori_loop(1, planes, add, 0)
+    total[...] = project(0, 0)
+    lax.fori_loop(1, 4, add, 0)
+    forward(3, 3)
+    lax.fori_loop(4, planes, add, 0)
     total[...] += project(0, 2)
-    for hop in (1, 2):
+    for hop in (1, 2, 3):
         total[...] += project(planes - hop, 2)
         total[...] += project(hop, 2)
-    forward(3, 3)
-    total[...] += project(planes - 3, 2)
-    total[...] += project(3, 2)
     forward(3, 4)
     total[...] += project(4, 2)
 

time: 126 us -> 125 us (level)
  no operation moved by 1% of the time
where the time goes in v3:
time: 125 us
  Pallas kernels  123 us (98%)
  local copies, waits for them, and re-layouts  1.87 us (1%)
    pallas_call x1, Pallas kernels, shards(): pl.pallas_call(functools.partial(layer_kernel, peers, planes, heads), out...  123 us

profile of v3, /device:TPU:1, one launch (start us, length us, event | category | flops | bytes accessed | tf_op | source)
XLA Modules:
  0.0 124.9 jit_solution(16371503793257884220)
XLA Ops:
  0.0 123.1 %shard_map.73 = bf16[512,512]{1,0:T(8,128)(2,1)} custom-call(bf16[512,512]{1,0:T(8,128)(2,1)} %q_hbm.1, bf16[512,512]{1,0:T(8,128)(2,1)} %k_hbm.1, bf16[512,512]{1,0:T(8,128)(2,1)} %v_hbm.1, s32[4,512]{1,0:T(4,128)} %route_hbm.1, s32[4,512]{1,0:T(4,128)} %members_hbm.1, s32[4,2,10]{2,1,0:T(2,128)} %pattern_hbm.1, bf16[64,512]{1,0:T(8,128)(2,1)} %bitcast.1), custom_call_target="tpu_custom_call" | custom-call | flops 7000000000 | bytes 3145728 | tf_op jit(solution)/shard_map/pallas_call | solution.py:410
  123.1 1.9 %copy.9 = bf16[512,512]{1,0:T(8,128)(2,1)} copy(bf16[512,512]{1,0:T(8,128)(2,1)} %shard_map.73) | data formatting | bytes 1048576
